TPU v7x, 128 devices: a whole 4x4x4 slice. The times are simulated.
128 devices in a mesh: loader: 4 (over z_hi, core), centers: 32 (over y, z_lo, x).
Axes of the slice: x: 4, y: 4, z: 4 (z_hi: 2, z_lo: 2; z = z_hi * 2 + z_lo), core: 2. Of those that a mesh axis runs over, the one named last changes fastest.
Arguments:
- pool: bfloat16 [32768, 256], P('loader'), may hold values from -6 to 6
- batch_index: int32 [2048], replicated, may hold values from 0 to 32767
- targets: float32 [16, 2048], replicated, may hold values from -6 to 6
- centers: bfloat16 [1048576, 256], P(('loader', 'centers')), may hold values from -6 to 6
- weights: float32 [16, 1048576], P(None, ('loader', 'centers')), may hold values from -1.8 to 1.8
- nys_index: int32 [8192], P(('loader', 'centers')), may hold values from 0 to 8191, as said below
- eigvecs: float32 [8192, 128], P(('loader', 'centers')), may hold values from -0.0625 to 0.0625
- damping: float32 [128], replicated, may hold values from 1 to 30
Outputs:
- new_weights: float32 [16, 1048576], P(None, ('loader', 'centers'))
- predictions: float32 [16, 2048], replicated
Inputs may be any that keep to these rules, and one draw needn't show every extreme that they name: `nys_index`: each device's block of 64 entries names distinct local rows of that device's own 8192 centers; entry k lies in [k * 128, (k + 1) * 128); the first is 0 and the last 8191.
All inputs are finite; a program needn't handle non-finite values.
Results may differ from a plain program's by a relative error of at most 0.0049.
Values may be sent and summed in bfloat16 or wider, within the bound.
No kernel may reach another device: no remote copies, remote signals or barrier semaphores. Data moves between devices by JAX's collectives and lax.ppermute only.
A program may use at most 256 MiB of HBM per device.

v0:
```python
import math
import jax
import jax.numpy as jnp
from jax import lax
from jax.sharding import PartitionSpec as P

D = 256


def pick_rows(pool, wanted):
    held = pool.shape[0]
    local = wanted - lax.axis_index("loader") * held
    owned = (local >= 0) & (local < held)
    rows = pool[jnp.clip(local, 0, held - 1)]
    return jnp.where(owned[:, None], rows, jnp.zeros_like(rows))


def body(pool, batch_index, targets, centers, weights, nys_index, eigvecs, damping):
    total_rows = batch_index.shape[0]
    share = total_rows // lax.axis_size("centers")
    mine = lax.dynamic_slice_in_dim(batch_index, lax.axis_index("centers") * share, share)
    summed = lax.psum(pick_rows(pool, mine), "loader").astype(jnp.float32).astype(jnp.bfloat16)
    batch = lax.all_gather(summed, "centers", axis=0, tiled=True)
    cen_sq = jnp.sum(centers.astype(jnp.float32) * centers.astype(jnp.float32), axis=1)
    width = min(512, total_rows)

    def tile(rows):
        row_sq = jnp.sum(rows.astype(jnp.float32) * rows.astype(jnp.float32), axis=1)
        cross = jnp.dot(rows, centers.T, preferred_element_type=jnp.float32)
        dist_sq = row_sq[:, None] + cen_sq[None, :] - 2.0 * cross
        return jnp.exp(-4.0 * jnp.sqrt(dist_sq) / math.sqrt(D)).astype(jnp.bfloat16)

    kern = lax.map(tile, batch.reshape(total_rows // width, width, batch.shape[1]))
    kern = kern.reshape(total_rows, centers.shape[0])
    w_half = weights.astype(jnp.bfloat16)
    partial_value = lax.dot_general(
        w_half, kern, (((1,), (1,)), ((), ())), preferred_element_type=jnp.float32
    )
    predictions = lax.psum(partial_value, ("loader", "centers"))
    resid = (predictions - targets).astype(jnp.bfloat16)
    grad = jnp.dot(resid, kern, preferred_element_type=jnp.float32)
    grad_nys = grad[:, nys_index]
    local_coeff = jnp.dot(
        grad_nys, eigvecs, precision=lax.Precision.HIGHEST, preferred_element_type=jnp.float32
    )
    coeff = lax.psum(local_coeff, ("loader", "centers"))
    delta = jnp.dot(
        coeff * damping[None, :],
        eigvecs.T,
        precision=lax.Precision.HIGHEST,
        preferred_element_type=jnp.float32,
    )
    fresh = weights - 2.0 * grad
    fresh = fresh.at[:, nys_index].add(2.0 * delta)
    return (fresh, predictions)


def solution(mesh):
    return jax.shard_map(
        body,
        mesh=mesh,
        in_specs=(
            P("loader", None),
            P(),
            P(),
            P(("loader", "centers"), None),
            P(None, ("loader", "centers")),
            P(("loader", "centers")),
            P(("loader", "centers"), None),
            P(),
        ),
        out_specs=(P(None, ("loader", "centers")), P()),
        check_vma=False,
    )
```

profile of v0, /device:TPU:1, one launch (start us, length us, event | category | flops | bytes accessed | tf_op | source)
XLA Modules:
  0.0 498.1 jit_solution(4399989665971109694)
XLA Ops:
  7.2 0.0 copy-start
  7.2 0.0 all-gather.2.cloned.1.call-start
  7.2 0.8 compare_select_fusion.1
  8.0 0.8 compare_and_fusion
  8.8 3.4 gather_fusion
  12.2 0.1 broadcast_select_fusion
  12.2 15.6 %psum.21 = bf16[64,256]{1,0:T(8,128)(2,1)} all-reduce(bf16[64,256]{1,0:T(8,128)(2,1)S(1)} %broadcast_select_fusion), channel_id=1, replica_groups=mesh['loader'=4,'centers'=32] {'loader'}, use_global_device_ids=true, to_apply=%region_0.1 | all-reduce | flops 16384 | bytes 65536 | tf_op jit(solution)/shard_map/psum | solution.py:22
  27.9 0.0 all-gather.2.cloned.1.call-update
  27.9 0.0 all-reduce.2.cloned.1.call-start
  28.0 0.7 compare_select_fusion
  28.6 3.3 multiply_reduce_fusion.1
  32.0 127.5 %all-gather.2.cloned.1.call-done = bf16[2048,256]{1,0:T(8,128)(2,1)} async-done(((bf16[64,256]{1,0:T(8,128)(2,1)}), bf16[2048,256]{1,0:T(8,128)(2,1)}) %all-gather.2.cloned.1.call-update) | async-done | bytes 1048592 | tf_op jit(solution)/shard_map/all_gather | solution.py:23
  159.5 0.0 copy-start.1
  159.5 58.4 %while.12 = (s32[]{:T(128)}, bf16[4,512,8192]{2,1,0:T(8,128)(2,1)}, bf16[4,512,256]{2,1,0:T(8,128)(2,1)}, f32[8192]{0:T(1024)S(1)}, bf16[8192,256]{1,0:T(8,128)(2,1)}, /*index=5*/s32[]{:T(128)}) while((s32[]{:T(128)}, bf16[4,512,8192]{2,1,0:T(8,128)(2,1)}, bf16[4,512,256]{2,1,0:T(8,128)(2,1)}, f32[8192]{0:T(1024)S(1)}, ...), condition=%wide.region_4.5_spmd, body=%wide.region_2.4_spmd.sunk | while | flops 2168847872 | bytes 13145161 | solution.py:33
  159.5 1.2 multiply_reduce_fusion.3
  160.6 13.5 %fusion.22 = bf16[4,512,8192]{2,1,0:T(8,128)(2,1)} fusion(bf16[4,512,8192]{2,1,0:T(8,128)(2,1)} %get-tuple-element.120, s32[]{:T(128)} %get-tuple-element.119, bf16[8192,256]{1,0:T(8,128)(2,1)} %get-tuple-element.129, f32[8192]{0:T(1024)S(1)} %get-tuple-element.128, f32[512]{0:T(512)S(1)} %multiply_reduce_fusion.3, ...), kind=kOutput, calls=%fused_computation.5.clone.1 | convolution fusion | flops 2168455168 | bytes 12880896 | tf_op jit(solution)/shard_map/while/body/eval_jaxpr/dot_general | solution.py:29
  174.1 1.1 multiply_reduce_fusion.3
  175.2 13.5 %fusion.22 = bf16[4,512,8192]{2,1,0:T(8,128)(2,1)} fusion(bf16[4,512,8192]{2,1,0:T(8,128)(2,1)} %get-tuple-element.120, s32[]{:T(128)} %get-tuple-element.119, bf16[8192,256]{1,0:T(8,128)(2,1)} %get-tuple-element.129, f32[8192]{0:T(1024)S(1)} %get-tuple-element.128, f32[512]{0:T(512)S(1)} %multiply_reduce_fusion.3, ...), kind=kOutput, calls=%fused_computation.5.clone.1 | convolution fusion | flops 2168455168 | bytes 12880896 | tf_op jit(solution)/shard_map/while/body/eval_jaxpr/dot_general | solution.py:29
  188.7 1.1 multiply_reduce_fusion.3
  189.8 13.5 %fusion.22 = bf16[4,512,8192]{2,1,0:T(8,128)(2,1)} fusion(bf16[4,512,8192]{2,1,0:T(8,128)(2,1)} %get-tuple-element.120, s32[]{:T(128)} %get-tuple-element.119, bf16[8192,256]{1,0:T(8,128)(2,1)} %get-tuple-element.129, f32[8192]{0:T(1024)S(1)} %get-tuple-element.128, f32[512]{0:T(512)S(1)} %multiply_reduce_fusion.3, ...), kind=kOutput, calls=%fused_computation.5.clone.1 | convolution fusion | flops 2168455168 | bytes 12880896 | tf_op jit(solution)/shard_map/while/body/eval_jaxpr/dot_general | solution.py:29
  203.3 1.1 multiply_reduce_fusion.3
  204.4 13.5 %fusion.22 = bf16[4,512,8192]{2,1,0:T(8,128)(2,1)} fusion(bf16[4,512,8192]{2,1,0:T(8,128)(2,1)} %get-tuple-element.120, s32[]{:T(128)} %get-tuple-element.119, bf16[8192,256]{1,0:T(8,128)(2,1)} %get-tuple-element.129, f32[8192]{0:T(1024)S(1)} %get-tuple-element.128, f32[512]{0:T(512)S(1)} %multiply_reduce_fusion.3, ...), kind=kOutput, calls=%fused_computation.5.clone.1 | convolution fusion | flops 2168455168 | bytes 12880896 | tf_op jit(solution)/shard_map/while/body/eval_jaxpr/dot_general | solution.py:29
  217.9 0.0 copy-done.1
  217.9 0.0 copy-start.3
  217.9 15.7 %convolution_bitcast_fusion = f32[16,2048]{1,0:T(8,128)} fusion(bf16[2048,8192]{1,0:T(8,128)(2,1)} %bitcast.28, f32[16,8192]{1,0:T(8,128)S(1)} %copy-done.1), kind=kOutput, calls=%fused_computation.11 | convolution fusion | flops 537001984 | bytes 34209792 | tf_op jit(solution)/shard_map/dot_general | solution.py:36
  233.6 0.0 all-reduce.2.cloned.1.call-update
  233.6 0.0 copy-start.4
  233.6 161.8 %all-reduce.2.cloned.1.call-done = f32[16,2048]{1,0:T(8,128)} async-done(((f32[16,2048]{1,0:T(8,128)}), f32[16,2048]{1,0:T(8,128)}) %all-reduce.2.cloned.1.call-update) | async-done | bytes 131088 | tf_op jit(solution)/shard_map/psum | solution.py:39
  395.4 0.0 copy-done.3
  395.4 0.0 copy-start.2
  395.4 14.8 %multiply_subtract_fusion = (f32[16,8192]{1,0:T(8,128)S(1)}, f32[16,8192]{1,0:T(8,128)S(1)}) fusion(f32[16,8192]{1,0:T(8,128)S(1)} %copy-done.1, bf16[2048,8192]{1,0:T(8,128)(2,1)} %bitcast.29, f32[16,2048]{1,0:T(8,128)} %all-reduce.2.cloned.1.call-done, f32[16,2048]{1,0:T(8,128)S(1)} %copy-done.3), kind=kOutput, calls=%fused_computation.14 | convolution fusion | flops 537198592 | bytes 35389440 | tf_op jit(solution)/shard_map/dot_general | solution.py:41
  410.3 2.6 copy.10
  412.9 2.8 gather_fusion.1
  415.7 0.0 copy-done
  415.7 0.2 fusion.10
  415.9 63.4 %psum.23 = f32[16,128]{1,0:T(8,128)S(1)} all-reduce(f32[16,128]{1,0:T(8,128)S(1)} %fusion.10), channel_id=1, replica_groups=mesh['loader'=4,'centers'=32] {'loader','centers'}, use_global_device_ids=true, to_apply=%region_6.7 | all-reduce | flops 2048 | bytes 16384 | tf_op jit(solution)/shard_map/psum | solution.py:46
  479.3 0.0 copy-done.4
  479.3 0.1 fusion.5
  479.4 0.1 copy.12
  479.5 2.6 copy.11
  482.1 4.9 scatter_fusion
  487.1 3.5 copy.13
  490.6 0.0 copy-done.2
  490.6 0.7 copy.25
  (3 shorter events, 0.0 us)
Async XLA Ops:
  7.2 408.5 %copy-start = (f32[64,128]{1,0:T(8,128)S(1)}, f32[64,128]{1,0:T(8,128)}, u32[]{:S(2)}) copy-start(f32[64,128]{1,0:T(8,128)} %param.16) | copy-start | bytes 98308
  7.2 152.3 %all-gather.2.cloned.1.call-start = ((), (), s32[]{:S(2)}) async-start(), calls=%async_computation | async-start | bytes 1081344 | tf_op jit(solution)/shard_map/all_gather | solution.py:23
  27.9 367.5 %all-reduce.2.cloned.1.call-start = ((), (), s32[]{:S(2)}) async-start(), calls=%async_computation.1 | async-start | bytes 262144 | tf_op jit(solution)/shard_map/psum | solution.py:39
  159.5 58.4 %copy-start.1 = (f32[16,8192]{1,0:T(8,128)S(1)}, f32[16,8192]{1,0:T(8,128)}, u32[]{:S(2)}) copy-start(f32[16,8192]{1,0:T(8,128)} %param.14) | copy-start | bytes 1572868
  217.9 177.5 %copy-start.3 = (f32[16,2048]{1,0:T(8,128)S(1)}, f32[16,2048]{1,0:T(8,128)}, u32[]{:S(2)}) copy-start(f32[16,2048]{1,0:T(8,128)} %param.12) | copy-start | bytes 393220
  233.6 245.7 %copy-start.4 = (f32[128]{0:T(128)S(1)}, f32[128]{0:T(128)}, u32[]{:S(2)}) copy-start(f32[128]{0:T(128)} %param.17) | copy-start | bytes 1540
  395.4 95.2 %copy-start.2 = (f32[16,2048]{1,0:T(8,128)S(1)}, f32[16,2048]{1,0:T(8,128)}, u32[]{:S(2)}) copy-start(f32[16,2048]{1,0:T(8,128)} %all-reduce.2.cloned.1.call-done) | copy-start | bytes 393220
Sparse Core Ops, SparseCore 0:
  28.0 131.4 all-gather.1
  233.7 161.6 all-reduce.1
where the time goes:
time: 499 us; the launch traced here: 498 us
  waiting for transfers between devices  289 us (58%)
  matrix products  84.8 us (17%)
  blocking collectives  79.1 us (16%)
  local copies, waits for them, and re-layouts  15.7 us (3%)
  other arithmetic  15 us (3%)
  between operations  14.1 us (3%)
    psum x1, waiting for transfers between devices, body(): predictions = lax.psum(partial_value, ('loader', 'centers'))  162 us
    all_gather x1, waiting for transfers between devices, body(): batch = lax.all_gather(summed, 'centers', axis=0, tiled=True)  128 us
    psum x1, blocking collectives, body(): coeff = lax.psum(local_coeff, ('loader', 'centers'))  63.4 us
    dot_general x4, matrix products, tile(): cross = jnp.dot(rows, centers.T, preferred_element_type=jnp.float32)  54 us
    dot_general x1, matrix products, body(): lax.dot_general(w_half, kern, (((1,), (1,)), ((), ())), preferred_element...  15.7 us
    psum x1, blocking collectives, body(): lax.psum(pick_rows(pool, mine), 'loader').astype(jnp.float32)  15.6 us
    dot_general x1, matrix products, body(): grad = jnp.dot(resid, kern, preferred_element_type=jnp.float32)  14.8 us
  transfers between devices with their start and end apart: 2, of which 2 were waited for; matrix products, arithmetic and copies ran while one was open for 1% of the time, Pallas kernels for 0%

commit v1 on v0

--- a/solution.py
+++ b/solution.py
@@ -5,6 +5,13 @@
 from jax.sharding import PartitionSpec as P
 
 D = 256
+
+
+def all_by_exchange(block, name, dim):
+    size = lax.axis_size(name)
+    blocks = jnp.stack([block for _ in range(size)])
+    blocks = lax.all_to_all(blocks, name, split_axis=0, concat_axis=0)
+    return jnp.concatenate(blocks, axis=dim)
 
 
 def pick_rows(pool, wanted):
@@ -20,7 +27,7 @@
     share = total_rows // lax.axis_size("centers")
     mine = lax.dynamic_slice_in_dim(batch_index, lax.axis_index("centers") * share, share)
     summed = lax.psum(pick_rows(pool, mine), "loader").astype(jnp.float32).astype(jnp.bfloat16)
-    batch = lax.all_gather(summed, "centers", axis=0, tiled=True)
+    batch = all_by_exchange(summed, "centers", 0)
     cen_sq = jnp.sum(centers.astype(jnp.float32) * centers.astype(jnp.float32), axis=1)
     width = min(512, total_rows)
 

time: 499 us -> 362 us (0.73)
  waiting for transfers between devices: 289 us -> 153 us
  starting transfers between devices: 0.08 us -> 7.69 us
    all_gather x1 -> x0, waiting for transfers between devices: 128 us -> none  [body(): batch = lax.all_gather(summed, 'centers', axis=0, tiled=True)]
    psum x1, waiting for transfers between devices: 162 us -> 143 us  [body(): predictions = lax.psum(partial_value, ('loader', 'centers'))]
    all_to_all x0 -> x1, waiting for transfers between devices: none -> 9.48 us  [all_by_exchange(): blocks = lax.all_to_all(blocks, name, split_axis=0, concat_axis=0)]
    all_to_all x0 -> x1, starting transfers between devices: none -> 7.65 us  [all_by_exchange(): blocks = lax.all_to_all(blocks, name, split_axis=0, concat_axis=0)]
where the time goes in v1:
time: 362 us
  waiting for transfers between devices  153 us (42%)
  matrix products  81.1 us (22%)
  blocking collectives  78.5 us (22%)
  local copies, waits for them, and re-layouts  16.8 us (5%)
  between operations  14.1 us (4%)
  other arithmetic  11.2 us (3%)
  starting transfers between devices  7.69 us (2%)
    psum x1, waiting for transfers between devices, body(): predictions = lax.psum(partial_value, ('loader', 'centers'))  143 us
    psum x1, blocking collectives, body(): coeff = lax.psum(local_coeff, ('loader', 'centers'))  63.4 us
    dot_general x4, matrix products, tile(): cross = jnp.dot(rows, centers.T, preferred_element_type=jnp.float32)  50.2 us
    dot_general x1, matrix products, body(): lax.dot_general(w_half, kern, (((1,), (1,)), ((), ())), preferred_element...  15.7 us
    psum x1, blocking collectives, body(): lax.psum(pick_rows(pool, mine), 'loader').astype(jnp.float32)  15 us
    dot_general x1, matrix products, body(): grad = jnp.dot(resid, kern, preferred_element_type=jnp.float32)  14.8 us
    all_to_all x1, waiting for transfers between devices, all_by_exchange(): blocks = lax.all_to_all(blocks, name, split_axis=0, concat_axis=0)  9.48 us
    all_to_all x1, starting transfers between devices, all_by_exchange(): blocks = lax.all_to_all(blocks, name, split_axis=0, concat_axis=0)  7.65 us
  transfers between devices with their start and end apart: 2, of which 2 were waited for; matrix products, arithmetic and copies ran while one was open for 1% of the time, Pallas kernels for 0%

profile of v1, /device:TPU:1, one launch (start us, length us, event | category | flops | bytes accessed | tf_op | source)
XLA Modules:
  0.0 361.8 jit_solution(13290372165352687629)
XLA Ops:
  7.2 0.0 copy-start
  7.2 0.8 compare_select_fusion.1
  8.0 0.8 compare_and_fusion
  8.7 3.4 gather_fusion
  12.1 0.1 broadcast_select_fusion
  12.2 15.0 %psum.21 = bf16[64,256]{1,0:T(8,128)(2,1)S(1)} all-reduce(bf16[64,256]{1,0:T(8,128)(2,1)S(1)} %broadcast_select_fusion), channel_id=1, replica_groups=mesh['loader'=4,'centers'=32] {'loader'}, use_global_device_ids=true, to_apply=%region_0.1 | all-reduce | flops 16384 | bytes 65536 | tf_op jit(solution)/shard_map/psum | solution.py:29
  27.2 1.1 stack.2
  28.3 7.6 %all-to-all-start = ((bf16[32,64,256]{2,1,0:T(8,128)(2,1)}), bf16[32,64,256]{2,1,0:T(8,128)(2,1)S(1)}, u32[]{:S(2)}, u32[]{:S(2)}) async-start(bf16[32,64,256]{2,1,0:T(8,128)(2,1)} %stack.2), calls=%async_computation | async-start | bytes 2097152 | tf_op jit(solution)/shard_map/all_to_all | solution.py:13
  36.0 0.0 all-reduce.2.cloned.1.call-start
  36.1 0.7 compare_select_fusion
  36.7 3.3 multiply_reduce_fusion.1
  40.1 9.5 %all-to-all-done = bf16[32,64,256]{2,1,0:T(8,128)(2,1)S(1)} async-done(((bf16[32,64,256]{2,1,0:T(8,128)(2,1)}), bf16[32,64,256]{2,1,0:T(8,128)(2,1)S(1)}, u32[]{:S(2)}, u32[]{:S(2)}) %all-to-all-start) | async-done | bytes 1048608 | tf_op jit(solution)/shard_map/all_to_all | solution.py:13
  49.5 0.0 copy-start.1
  49.5 50.8 %while.12 = (s32[]{:T(128)}, bf16[4,512,8192]{2,1,0:T(8,128)(2,1)}, bf16[4,512,256]{2,1,0:T(8,128)(2,1)S(1)}, f32[8192]{0:T(1024)S(1)}, bf16[8192,256]{1,0:T(8,128)(2,1)}, /*index=5*/s32[]{:T(128)}) while((s32[]{:T(128)}, bf16[4,512,8192]{2,1,0:T(8,128)(2,1)}, bf16[4,512,256]{2,1,0:T(8,128)(2,1)S(1)}, f32[8192]{0:T(1024)S(1)}, ...), condition=%wide.region_4.5_spmd, body=%wide.region_2.4_spmd.sunk | while | flops 2168847872 | bytes 13145161 | solution.py:40
  49.5 0.1 multiply_reduce_fusion.3
  49.7 12.6 %fusion.22 = bf16[4,512,8192]{2,1,0:T(8,128)(2,1)} fusion(bf16[4,512,8192]{2,1,0:T(8,128)(2,1)} %get-tuple-element.120, s32[]{:T(128)} %get-tuple-element.119, bf16[8192,256]{1,0:T(8,128)(2,1)} %get-tuple-element.129, f32[8192]{0:T(1024)S(1)} %get-tuple-element.128, f32[512]{0:T(512)S(1)} %multiply_reduce_fusion.3, ...), kind=kOutput, calls=%fused_computation.5.clone.1 | convolution fusion | flops 2168455168 | bytes 12880896 | tf_op jit(solution)/shard_map/while/body/eval_jaxpr/dot_general | solution.py:36
  62.3 0.1 multiply_reduce_fusion.3
  62.4 12.6 %fusion.22 = bf16[4,512,8192]{2,1,0:T(8,128)(2,1)} fusion(bf16[4,512,8192]{2,1,0:T(8,128)(2,1)} %get-tuple-element.120, s32[]{:T(128)} %get-tuple-element.119, bf16[8192,256]{1,0:T(8,128)(2,1)} %get-tuple-element.129, f32[8192]{0:T(1024)S(1)} %get-tuple-element.128, f32[512]{0:T(512)S(1)} %multiply_reduce_fusion.3, ...), kind=kOutput, calls=%fused_computation.5.clone.1 | convolution fusion | flops 2168455168 | bytes 12880896 | tf_op jit(solution)/shard_map/while/body/eval_jaxpr/dot_general | solution.py:36
  75.0 0.1 multiply_reduce_fusion.3
  75.1 12.6 %fusion.22 = bf16[4,512,8192]{2,1,0:T(8,128)(2,1)} fusion(bf16[4,512,8192]{2,1,0:T(8,128)(2,1)} %get-tuple-element.120, s32[]{:T(128)} %get-tuple-element.119, bf16[8192,256]{1,0:T(8,128)(2,1)} %get-tuple-element.129, f32[8192]{0:T(1024)S(1)} %get-tuple-element.128, f32[512]{0:T(512)S(1)} %multiply_reduce_fusion.3, ...), kind=kOutput, calls=%fused_computation.5.clone.1 | convolution fusion | flops 2168455168 | bytes 12880896 | tf_op jit(solution)/shard_map/while/body/eval_jaxpr/dot_general | solution.py:36
  87.7 0.1 multiply_reduce_fusion.3
  87.8 12.5 %fusion.22 = bf16[4,512,8192]{2,1,0:T(8,128)(2,1)} fusion(bf16[4,512,8192]{2,1,0:T(8,128)(2,1)} %get-tuple-element.120, s32[]{:T(128)} %get-tuple-element.119, bf16[8192,256]{1,0:T(8,128)(2,1)} %get-tuple-element.129, f32[8192]{0:T(1024)S(1)} %get-tuple-element.128, f32[512]{0:T(512)S(1)} %multiply_reduce_fusion.3, ...), kind=kOutput, calls=%fused_computation.5.clone.1 | convolution fusion | flops 2168455168 | bytes 12880896 | tf_op jit(solution)/shard_map/while/body/eval_jaxpr/dot_general | solution.py:36
  100.4 0.0 copy-done.1
  100.4 0.0 copy-start.3
  100.4 15.7 %convolution_bitcast_fusion = f32[16,2048]{1,0:T(8,128)} fusion(bf16[2048,8192]{1,0:T(8,128)(2,1)} %bitcast.28, f32[16,8192]{1,0:T(8,128)S(1)} %copy-done.1), kind=kOutput, calls=%fused_computation.11 | convolution fusion | flops 537001984 | bytes 34209792 | tf_op jit(solution)/shard_map/dot_general | solution.py:43
  116.0 0.0 all-reduce.2.cloned.1.call-update
  116.1 0.0 copy-start.4
  116.1 143.0 %all-reduce.2.cloned.1.call-done = f32[16,2048]{1,0:T(8,128)} async-done(((f32[16,2048]{1,0:T(8,128)}), f32[16,2048]{1,0:T(8,128)}) %all-reduce.2.cloned.1.call-update) | async-done | bytes 131088 | tf_op jit(solution)/shard_map/psum | solution.py:46
  259.1 0.0 copy-done.3
  259.1 0.0 copy-start.2
  259.1 14.8 %multiply_subtract_fusion = (f32[16,8192]{1,0:T(8,128)S(1)}, f32[16,8192]{1,0:T(8,128)S(1)}) fusion(f32[16,8192]{1,0:T(8,128)S(1)} %copy-done.1, bf16[2048,8192]{1,0:T(8,128)(2,1)} %bitcast.29, f32[16,2048]{1,0:T(8,128)} %all-reduce.2.cloned.1.call-done, f32[16,2048]{1,0:T(8,128)S(1)} %copy-done.3), kind=kOutput, calls=%fused_computation.14 | convolution fusion | flops 537198592 | bytes 35389440 | tf_op jit(solution)/shard_map/dot_general | solution.py:48
  274.0 2.6 copy.10
  276.6 2.8 gather_fusion.1
  279.3 0.0 copy-done
  279.3 0.2 fusion.10
  279.5 63.4 %psum.23 = f32[16,128]{1,0:T(8,128)S(1)} all-reduce(f32[16,128]{1,0:T(8,128)S(1)} %fusion.10), channel_id=1, replica_groups=mesh['loader'=4,'centers'=32] {'loader','centers'}, use_global_device_ids=true, to_apply=%region_6.7 | all-reduce | flops 2048 | bytes 16384 | tf_op jit(solution)/shard_map/psum | solution.py:53
  343.0 0.0 copy-done.4
  343.0 0.1 fusion.5
  343.1 0.1 copy.12
  343.2 2.6 copy.11
  345.8 4.9 %scatter_fusion = f32[16,8192]{0,1:T(8,128)} fusion(f32[16,8192]{0,1:T(8,128)} %copy.11, s32[64]{0:T(128)S(1)} %compare_select_fusion, f32[64,16]{1,0:T(8,128)S(1)} %copy.12), kind=kCustom, calls=%fused_computation.2 | custom fusion | flops 1024 | bytes 12544 | tf_op jit(solution)/shard_map/scatter-add | solution.py:61
  350.8 3.5 copy.13
  354.3 0.0 copy-done.2
  354.3 0.7 copy.25
  (3 shorter events, 0.0 us)
Async XLA Ops:
  7.2 272.2 %copy-start = (f32[64,128]{1,0:T(8,128)S(1)}, f32[64,128]{1,0:T(8,128)}, u32[]{:S(2)}) copy-start(f32[64,128]{1,0:T(8,128)} %param.16) | copy-start | bytes 98308
  28.3 21.2 %all-to-all-start = ((bf16[32,64,256]{2,1,0:T(8,128)(2,1)}), bf16[32,64,256]{2,1,0:T(8,128)(2,1)S(1)}, u32[]{:S(2)}, u32[]{:S(2)}) async-start(bf16[32,64,256]{2,1,0:T(8,128)(2,1)} %stack.2), calls=%async_computation | async-start | bytes 2097152 | tf_op jit(solution)/shard_map/all_to_all | solution.py:13
  36.0 223.1 %all-reduce.2.cloned.1.call-start = ((), (), s32[]{:S(2)}) async-start(), calls=%async_computation.1 | async-start | bytes 262144 | tf_op jit(solution)/shard_map/psum | solution.py:46
  49.5 50.8 %copy-start.1 = (f32[16,8192]{1,0:T(8,128)S(1)}, f32[16,8192]{1,0:T(8,128)}, u32[]{:S(2)}) copy-start(f32[16,8192]{1,0:T(8,128)} %param.14) | copy-start | bytes 1572868
  100.4 158.7 %copy-start.3 = (f32[16,2048]{1,0:T(8,128)S(1)}, f32[16,2048]{1,0:T(8,128)}, u32[]{:S(2)}) copy-start(f32[16,2048]{1,0:T(8,128)} %param.12) | copy-start | bytes 393220
  116.1 226.9 %copy-start.4 = (f32[128]{0:T(128)S(1)}, f32[128]{0:T(128)}, u32[]{:S(2)}) copy-start(f32[128]{0:T(128)} %param.17) | copy-start | bytes 1540
  259.1 95.2 %copy-start.2 = (f32[16,2048]{1,0:T(8,128)S(1)}, f32[16,2048]{1,0:T(8,128)}, u32[]{:S(2)}) copy-start(f32[16,2048]{1,0:T(8,128)} %all-reduce.2.cloned.1.call-done) | copy-start | bytes 393220
Sparse Core Ops, SparseCore 0:
  116.2 142.8 all-reduce.1
